TPU v7x, 256 devices: a whole 4x4x8 slice. The times are simulated.
256 devices in a mesh: gy: 16 (over z, y_lo), gz: 16 (over x, y_hi, core).
Axes of the slice: x: 4, y: 4 (y_hi: 2, y_lo: 2; y = y_hi * 2 + y_lo), z: 8, core: 2. Of those that a mesh axis runs over, the one named last changes fastest.
Arguments:
- wave_field: float32 [2, 2, 256, 256, 256], P(None, None, 'gy', 'gz'), may hold values from -2.5 to 2.5
- trap_field: float32 [256, 256, 256], P('gy', 'gz'), may hold values from 0 to 1.5
Outputs:
- wave_next: float32 [2, 2, 256, 256, 256], P(None, None, 'gy', 'gz')
- momentum_image: float32 [256, 256, 256], P('gy', 'gz')
All inputs are finite; a program needn't handle non-finite values.
Results may differ from a plain program's by a relative error of at most 0.0003.
Values sent between devices are 32-bit elements; how exact they have to be, the bound alone decides.
A program may use at most 128 MiB of HBM per device.

v0:
```python
import math

import jax
import jax.numpy as jnp
import numpy as np
from jax import lax
from jax.experimental import pallas as pl
from jax.experimental.pallas import tpu as pltpu
from jax.sharding import PartitionSpec as P

MESH = pl.DeviceIdType.MESH

hopping = 1.5
time_step = 0.1
rabi_rate = 0.8
inter_self_first = 0.1
inter_cross = 0.06
inter_self_second = 0.08

CHUNKS = 4


def rotation(angle):
    c, s = np.cos(angle), np.sin(angle)
    return np.stack([np.stack([c, s]), np.stack([-s, c])])


def in_two(table):
    table = table.astype(np.float32)
    high = table.astype(jnp.bfloat16)
    low = (table - high.astype(np.float32)).astype(jnp.bfloat16)
    return np.stack([high, low])


def tables(n):
    size, half = n * n, n // 2
    i = np.arange(size)
    full = rotation(2.0 * np.pi * ((i[:, None] * i[None, :]) % size) / size)
    one = full.reshape(2, 2, n, 2, half, size).transpose(3, 2, 0, 4, 1, 5)
    one = one.reshape(2, size, 2 * size)
    j = np.arange(n)
    small = rotation(2.0 * np.pi * ((j[:, None] * j[None, :]) % n) / n)
    two = np.einsum("opay,zw->aozpyw", small, np.eye(n)).reshape(2 * size, 2 * size)
    three = full.reshape(2, 2, size, n, n).transpose(0, 2, 3, 1, 4).reshape(2 * size, 2 * size)
    turn = 2.0 * np.pi * (j[:, None] * j[None, :]) / size
    turn = np.repeat(turn, n, axis=1)
    twiddle = np.stack([np.cos(turn), np.sin(turn)], axis=1).astype(np.float32)
    return in_two(one), in_two(two), in_two(three), twiddle


def fourier(values):
    count = len(values)
    if count == 1:
        return values
    even, odd = fourier(values[0::2]), fourier(values[1::2])
    first, second = [], []
    for k in range(count // 2):
        (er, ei), (r, i) = even[k], odd[k]
        if k == 0:
            tr, ti = r, i
        elif 4 * k == count:
            tr, ti = i, -r
        else:
            c, s = math.cos(2.0 * math.pi * k / count), math.sin(2.0 * math.pi * k / count)
            if 8 * k == count:
                tr, ti = c * (r + i), c * (i - r)
            elif 8 * k == 3 * count:
                tr, ti = s * (i - r), -s * (r + i)
            else:
                tr, ti = c * r + s * i, c * i - s * r
        first.append((er + tr, ei + ti))
        second.append((er - tr, ei - ti))
    return first + second


def split(value):
    high = value.astype(jnp.bfloat16)
    return high, (value - high.astype(jnp.float32)).astype(jnp.bfloat16)


def product(table, high, low, dims):
    def dot(a, b):
        return lax.dot_general(a, b, (dims, ((), ())), preferred_element_type=jnp.float32)

    return dot(table[0], high) + (dot(table[0], low) + dot(table[1], high))


NT = ((1,), (1,))
NN = ((1,), (0,))


def kernel(
    n, wave_hbm, trap_hbm, one_hbm, two_hbm, three_hbm, twiddle_hbm,
    next_hbm, image_ref,
    state, face_out, face_in, trap, wave_next, field, one, two, three, twiddle,
    sent_y, got_y, mixed, sent_z, got_z,
    load_sem, store_sem, halo_send, halo_recv, y_send, y_recv, z_send, z_recv,
):
    size, half = n * n, n // 2
    gy, gz = lax.axis_index("gy"), lax.axis_index("gz")

    def in_y(d):
        return (lax.rem(gy + d, n), gz)

    def in_z(d):
        return (gy, lax.rem(gz + d, n))

    barrier = pltpu.get_barrier_semaphore()

    def greet(d, carry):
        pl.semaphore_signal(barrier, inc=1, device_id=in_y(d), device_id_type=MESH)
        pl.semaphore_signal(barrier, inc=1, device_id=in_z(d), device_id_type=MESH)
        return carry

    lax.fori_loop(1, n, greet, 0)

    loads = [
        pltpu.make_async_copy(wave_hbm, state.at[0, :, pl.ds(1, n)], load_sem.at[0]),
        pltpu.make_async_copy(trap_hbm, trap, load_sem.at[1]),
        pltpu.make_async_copy(one_hbm, one, load_sem.at[2]),
        pltpu.make_async_copy(two_hbm, two, load_sem.at[3]),
        pltpu.make_async_copy(three_hbm, three, load_sem.at[4]),
        pltpu.make_async_copy(twiddle_hbm, twiddle, load_sem.at[5]),
    ]
    for load in loads:
        load.start()
    loads[0].wait()

    def y_faces(s):
        up = pltpu.make_async_remote_copy(
            src_ref=state.at[s, :, pl.ds(n, 1)], dst_ref=state.at[s, :, pl.ds(0, 1)],
            send_sem=halo_send.at[s, 0], recv_sem=halo_recv.at[s, 0],
            device_id=in_y(1), device_id_type=MESH,
        )
        down = pltpu.make_async_remote_copy(
            src_ref=state.at[s, :, pl.ds(1, 1)], dst_ref=state.at[s, :, pl.ds(n + 1, 1)],
            send_sem=halo_send.at[s, 1], recv_sem=halo_recv.at[s, 1],
            device_id=in_y(n - 1), device_id_type=MESH,
        )
        return up, down

    def z_faces(s):
        up = pltpu.make_async_remote_copy(
            src_ref=face_out.at[s, 1], dst_ref=face_in.at[s, 0],
            send_sem=halo_send.at[s, 2], recv_sem=halo_recv.at[s, 2],
            device_id=in_z(1), device_id_type=MESH,
        )
        down = pltpu.make_async_remote_copy(
            src_ref=face_out.at[s, 0], dst_ref=face_in.at[s, 1],
            send_sem=halo_send.at[s, 3], recv_sem=halo_recv.at[s, 3],
            device_id=in_z(n - 1), device_id_type=MESH,
        )
        return up, down

    pl.semaphore_wait(barrier, 2 * (n - 1))
    for copy in y_faces(0):
        copy.start()

    def first_faces(y, carry):
        for i in range(4):
            plane = state[0, i, y + 1]
            face_out[0, 0, i, pl.ds(y, 1), :] = plane[0:1]
            face_out[0, 1, i, pl.ds(y, 1), :] = plane[n - 1 : n]
        return carry

    lax.fori_loop(0, n, first_faces, 0)
    for copy in z_faces(0):
        copy.start()
    loads[1].wait()

    row = lax.broadcasted_iota(jnp.int32, (n, size), 0)

    def slope(s, y):
        center = [state[s, i, y + 1] for i in range(4)]
        density = [
            center[0] * center[0] + center[1] * center[1],
            center[2] * center[2] + center[3] * center[3],
        ]
        base = trap[y]
        level = [
            base + inter_self_first * density[0] + inter_cross * density[1],
            base + inter_cross * density[0] + inter_self_second * density[1],
        ]
        applied = []
        for i in range(4):
            mid = center[i]
            beside = state[s, i, y + 2] + state[s, i, y]
            before = face_in[s, 0, i, pl.ds(y, 1), :]
            after = face_in[s, 1, i, pl.ds(y, 1), :]
            beside += jnp.where(row == 0, before, pltpu.roll(mid, 1, 0))
            beside += jnp.where(row == n - 1, after, pltpu.roll(mid, n - 1, 0))
            beside += pltpu.roll(mid, 1, 1) + pltpu.roll(mid, size - 1, 1)
            applied.append(
                level[i // 2] * mid - hopping * beside - 0.5 * rabi_rate * center[(i + 2) % 4]
            )
        return [applied[1], -applied[0], applied[3], -applied[2]]

    for s in range(4):
        for copy in y_faces(s) + z_faces(s):
            copy.wait_recv()

        if s < 3:
            step = (0.5 * time_step, 0.5 * time_step, time_step)[s]

            def plane(y, s=s, step=step):
                for i, change in enumerate(slope(s, y)):
                    new = state[0, i, y + 1] + step * change
                    state[s + 1, i, y + 1] = new
                    face_out[s + 1, 0, i, pl.ds(y, 1), :] = new[0:1]
                    face_out[s + 1, 1, i, pl.ds(y, 1), :] = new[n - 1 : n]

            def outer(j, carry):
                plane(j * (n - 1))
                return carry

            def inner(y, carry):
                plane(y)
                return carry

            lax.fori_loop(0, 2, outer, 0)
            for copy in y_faces(s + 1):
                copy.start()
            lax.fori_loop(1, n - 1, inner, 0)
            for copy in z_faces(s + 1):
                copy.start()
        else:

            def last(y, carry):
                for i, change in enumerate(slope(3, y)):
                    kept = (
                        state[1, i, y + 1] + state[3, i, y + 1] - state[0, i, y + 1]
                        + 2.0 * state[2, i, y + 1]
                    )
                    new = kept * (1.0 / 3.0) + (time_step / 6.0) * change
                    wave_next[i, y] = new
                    high, low = split(new)
                    rows = pl.ds(pl.multiple_of(y * n, n), n)
                    field[0, i // 2, rows, (i % 2) * size : (i % 2 + 1) * size] = high
                    field[1, i // 2, rows, (i % 2) * size : (i % 2 + 1) * size] = low
                return carry

            lax.fori_loop(0, n, last, 0)

    store = pltpu.make_async_copy(wave_next, next_hbm, store_sem)
    store.start()

    def y_copy(ch, d):
        return pltpu.make_async_remote_copy(
            src_ref=sent_y.at[ch, lax.rem(gy + d, n)], dst_ref=got_y.at[ch, gy],
            send_sem=y_send.at[ch, d], recv_sem=y_recv.at[ch, d],
            device_id=in_y(d), device_id_type=MESH,
        )

    def z_copy(ch, d):
        return pltpu.make_async_remote_copy(
            src_ref=sent_z.at[ch, lax.rem(gz + d, n)], dst_ref=got_z.at[ch, gz],
            send_sem=z_send.at[ch, d], recv_sem=z_recv.at[ch, d],
            device_id=in_z(d), device_id_type=MESH,
        )

    def start_all(copy, ch):
        def one_start(j, carry):
            away = j // 2 + 1
            copy(ch, lax.rem(n + away * (1 - 2 * (j % 2)), n)).start()
            return carry

        lax.fori_loop(0, n - 1, one_start, 0)

    def arrived(copy, ch):
        def one_wait(d, carry):
            copy(ch, d).wait_recv()
            return carry

        lax.fori_loop(1, n, one_wait, 0)

    loads[2].wait()

    def along_x(ch, carry):
        c, h = ch % 2, ch // 2
        out = product((one[0, h], one[1, h]), field[0, c], field[1, c], NT)
        sent_y[ch] = out.reshape(n, n, size)
        start_all(y_copy, ch)
        got_y[ch, gy] = sent_y[ch, gy]
        return carry

    lax.fori_loop(0, CHUNKS, along_x, 0)

    loads[3].wait()
    loads[5].wait()

    def along_y(ch, carry):
        arrived(y_copy, ch)
        lanes = size // 2
        for part in range(2):
            at = slice(part * lanes, (part + 1) * lanes)
            values = [(got_y[ch, s, 0:half, at], got_y[ch, s, half:n, at]) for s in range(n)]
            values = fourier(values)
            for b in range(0, n, 2):
                turned = []
                for k in (b, b + 1):
                    (re, im), cos, sin = values[k], twiddle[k, 0:1, at], twiddle[k, 1:2, at]
                    turned.append((re * cos + im * sin, im * cos - re * sin))
                for p in range(2):
                    both = jnp.concatenate([turned[0][p], turned[1][p]], axis=0)
                    high, low = split(both)
                    to = slice(p * size + part * lanes, p * size + (part + 1) * lanes)
                    mixed[0, b * half : (b + 2) * half, to] = high
                    mixed[1, b * half : (b + 2) * half, to] = low
        out = product((two[0], two[1]), mixed[0], mixed[1], NT)
        sent_z[ch] = out.reshape(n, 2 * n, size // 2)
        start_all(z_copy, ch)
        got_z[ch, gz] = sent_z[ch, gz]
        return carry

    lax.fori_loop(0, CHUNKS, along_y, 0)

    loads[4].wait()

    def along_z(h, carry):
        power = None
        for c in range(2):
            ch = 2 * h + c
            arrived(z_copy, ch)
            high, low = split(got_z[ch].reshape(2 * size, size // 2))
            out = product((three[0], three[1]), high, low, NN)
            re, im = out[:size], out[size:]
            new = re * re + im * im
            power = new if power is None else power + new
        image_ref[h] = (power * (1.0 / float(size**3))).T
        return carry

    lax.fori_loop(0, 2, along_z, 0)

    for s in range(4):
        for copy in y_faces(s) + z_faces(s):
            copy.wait_send()

    def sent(j, carry):
        for ch in range(CHUNKS):
            y_copy(ch, j).wait_send()
            z_copy(ch, j).wait_send()
        return carry

    lax.fori_loop(1, n, sent, 0)
    store.wait()


def solution(mesh):
    n = mesh.shape["gy"]
    size, half = n * n, n // 2
    arrays = tables(n)

    def body(wave_field, trap_field):
        f32, bf16 = jnp.float32, jnp.bfloat16
        dma = pltpu.SemaphoreType.DMA
        wave_next, image = pl.pallas_call(
            lambda *refs: kernel(n, *refs),
            out_shape=(
                jax.ShapeDtypeStruct((4, n, n, size), f32),
                jax.ShapeDtypeStruct((2, size // 2, size), f32),
            ),
            in_specs=[pl.BlockSpec(memory_space=pl.ANY)] * 6,
            out_specs=(
                pl.BlockSpec(memory_space=pl.ANY),
                pl.BlockSpec(memory_space=pltpu.VMEM),
            ),
            scratch_shapes=[
                pltpu.VMEM((4, 4, n + 2, n, size), f32),
                pltpu.VMEM((4, 2, 4, n, size), f32),
                pltpu.VMEM((4, 2, 4, n, size), f32),
                pltpu.VMEM((n, n, size), f32),
                pltpu.VMEM((4, n, n, size), f32),
                pltpu.VMEM((2, 2, size, 2 * size), bf16),
                pltpu.VMEM((2, 2, size, 2 * size), bf16),
                pltpu.VMEM((2, 2 * size, 2 * size), bf16),
                pltpu.VMEM((2, 2 * size, 2 * size), bf16),
                pltpu.VMEM((n, 2, size), f32),
                pltpu.VMEM((CHUNKS, n, n, size), f32),
                pltpu.VMEM((CHUNKS, n, n, size), f32),
                pltpu.VMEM((2, size // 2, 2 * size), bf16),
                pltpu.VMEM((CHUNKS, n, 2 * n, size // 2), f32),
                pltpu.VMEM((CHUNKS, n, 2 * n, size // 2), f32),
                dma((6,)),
                dma(()),
                dma((4, 4)),
                dma((4, 4)),
                dma((CHUNKS, n)),
                dma((CHUNKS, n)),
                dma((CHUNKS, n)),
                dma((CHUNKS, n)),
            ],
            compiler_params=pltpu.CompilerParams(
                collective_id=0, has_side_effects=True, vmem_limit_bytes=48 * 1024 * 1024
            ),
        )(wave_field.reshape(4, n, n, size), trap_field, *(jnp.asarray(a) for a in arrays))
        image = image.reshape(2, n, half, size).transpose(0, 2, 1, 3).reshape(n, n, size)
        return wave_next.reshape(2, 2, n, n, size), image

    return jax.shard_map(
        body,
        mesh=mesh,
        in_specs=(P(None, None, "gy", "gz", None), P("gy", "gz", None)),
        out_specs=(P(None, None, "gy", "gz", None), P("gy", "gz", None)),
        check_vma=False,
    )
```

profile of v0, /device:TPU:1, one launch (start us, length us, event | category | flops | bytes accessed | tf_op | source)
XLA Modules:
  0.0 84.0 jit_solution(7899311539723468742)
XLA Ops:
  0.6 0.0 copy-start
  0.6 1.2 %copy-done = f32[2,2,16,16,256]{4,3,2,1,0:T(8,128)S(1)} copy-done((f32[2,2,16,16,256]{4,3,2,1,0:T(8,128)S(1)}, f32[2,2,16,16,256]{4,3,2,1,0:T(8,128)}, u32[]{:S(2)}) %copy-start) | copy-done | bytes 1048600
  1.9 0.0 copy-start.1
  1.9 1.2 %copy-done.1 = bf16[2,512,512]{2,1,0:T(8,128)(2,1)S(1)} copy-done((bf16[2,512,512]{2,1,0:T(8,128)(2,1)S(1)}, bf16[2,512,512]{2,1,0:T(8,128)(2,1)}, u32[]{:S(2)}) %copy-start.1) | copy-done | bytes 1048600
  3.1 0.0 copy-start.2
  3.1 1.2 %copy-done.2 = bf16[2,512,512]{2,1,0:T(8,128)(2,1)S(1)} copy-done((bf16[2,512,512]{2,1,0:T(8,128)(2,1)S(1)}, bf16[2,512,512]{2,1,0:T(8,128)(2,1)}, u32[]{:S(2)}) %copy-start.2) | copy-done | bytes 1048600
  4.3 0.0 copy-start.3
  4.3 1.2 %copy-done.3 = bf16[2,2,256,512]{3,2,1,0:T(8,128)(2,1)S(1)} copy-done((bf16[2,2,256,512]{3,2,1,0:T(8,128)(2,1)S(1)}, bf16[2,2,256,512]{3,2,1,0:T(8,128)(2,1)}, u32[]{:S(2)}) %copy-start.3) | copy-done | bytes 1048600
  5.5 0.0 copy-start.4
  5.5 0.9 %copy-done.4 = f32[16,16,256]{2,1,0:T(8,128)S(1)} copy-done((f32[16,16,256]{2,1,0:T(8,128)S(1)}, f32[16,16,256]{2,1,0:T(8,128)}, u32[]{:S(2)}) %copy-start.4) | copy-done | bytes 262168
  6.5 0.0 copy-start.5
  6.5 0.8 copy-done.5
  7.2 75.0 %shard_map.77 = (f32[4,16,16,256]{3,2,1,0:T(8,128)S(1)}, f32[2,128,256]{2,1,0:T(8,128)S(1)}) custom-call(f32[4,16,16,256]{3,2,1,0:T(8,128)S(1)} %bitcast.6, f32[16,16,256]{2,1,0:T(8,128)S(1)} %copy-done.4, bf16[2,2,256,512]{3,2,1,0:T(8,128)(2,1)S(1)} %copy-done.3, bf16[2,512,512]{2,1,0:T(8,128)(2,1)S(1)} %copy-done.2, bf16[2,512,512]{2,1,0:T(8,128)(2,1)S(1)} %copy-done.1, ...), custom_call_target="tpu_custom_call" | custom-call | tf_op jit(solution)/shard_map/pallas_call | solution.py:356
  82.2 0.8 copy.8
  83.0 1.0 %copy.10 = f32[2,2,16,16,256]{4,3,2,1,0:T(8,128)} copy(f32[2,2,16,16,256]{4,3,2,1,0:T(8,128)S(1)} %bitcast.7) | data formatting | bytes 2097152
Async XLA Ops:
  0.6 1.2 %copy-start = (f32[2,2,16,16,256]{4,3,2,1,0:T(8,128)S(1)}, f32[2,2,16,16,256]{4,3,2,1,0:T(8,128)}, u32[]{:S(2)}) copy-start(f32[2,2,16,16,256]{4,3,2,1,0:T(8,128)} %param.6) | copy-start | bytes 3145732
  1.9 1.2 %copy-start.1 = (bf16[2,512,512]{2,1,0:T(8,128)(2,1)S(1)}, bf16[2,512,512]{2,1,0:T(8,128)(2,1)}, u32[]{:S(2)}) copy-start(bf16[2,512,512]{2,1,0:T(8,128)(2,1)} %constant.10.clone.refs_4_) | copy-start | bytes 3145732
  3.1 1.2 %copy-start.2 = (bf16[2,512,512]{2,1,0:T(8,128)(2,1)S(1)}, bf16[2,512,512]{2,1,0:T(8,128)(2,1)}, u32[]{:S(2)}) copy-start(bf16[2,512,512]{2,1,0:T(8,128)(2,1)} %constant.9.clone.refs_3_) | copy-start | bytes 3145732
  4.3 1.2 %copy-start.3 = (bf16[2,2,256,512]{3,2,1,0:T(8,128)(2,1)S(1)}, bf16[2,2,256,512]{3,2,1,0:T(8,128)(2,1)}, u32[]{:S(2)}) copy-start(bf16[2,2,256,512]{3,2,1,0:T(8,128)(2,1)} %constant.8.clone.refs_2_) | copy-start | bytes 3145732
  5.5 0.9 %copy-start.4 = (f32[16,16,256]{2,1,0:T(8,128)S(1)}, f32[16,16,256]{2,1,0:T(8,128)}, u32[]{:S(2)}) copy-start(f32[16,16,256]{2,1,0:T(8,128)} %refs_1_.1) | copy-start | bytes 786436
  6.5 0.8 copy-start.5
where the time goes:
time: 84.3 us; the launch traced here: 84 us
  Pallas kernels  75 us (89%)
  local copies, waits for them, and re-layouts  8.35 us (10%)
    pallas_call x1, Pallas kernels, body(): pl.pallas_call(lambda *refs: kernel(n, *refs), out_shape=(jax.ShapeDtypeS...  75 us
    unnamed x13, local copies, waits for them, and re-layouts  7.57 us

commit v1 on v0

--- a/solution.py
+++ b/solution.py
@@ -92,11 +92,13 @@
 def kernel(
     n, wave_hbm, trap_hbm, one_hbm, two_hbm, three_hbm, twiddle_hbm,
     next_hbm, image_ref,
-    state, face_out, face_in, trap, wave_next, field, one, two, three, twiddle,
-    sent_y, got_y, mixed, sent_z, got_z,
+    state0, state1, state2, state3, out0, out1, out2, out3, in0, in1, in2, in3, trap, wave_next, field, one, two, three, twiddle,
+    sent_y, got_y, mixed, sent_z, got_z, power,
     load_sem, store_sem, halo_send, halo_recv, y_send, y_recv, z_send, z_recv,
 ):
     size, half = n * n, n // 2
+    state = (state0, state1, state2, state3)
+    face_out, face_in = (out0, out1, out2, out3), (in0, in1, in2, in3)
     gy, gz = lax.axis_index("gy"), lax.axis_index("gz")
 
     def in_y(d):
@@ -105,144 +107,130 @@
     def in_z(d):
         return (gy, lax.rem(gz + d, n))
 
-    barrier = pltpu.get_barrier_semaphore()
-
-    def greet(d, carry):
-        pl.semaphore_signal(barrier, inc=1, device_id=in_y(d), device_id_type=MESH)
-        pl.semaphore_signal(barrier, inc=1, device_id=in_z(d), device_id_type=MESH)
-        return carry
-
-    lax.fori_loop(1, n, greet, 0)
-
     loads = [
-        pltpu.make_async_copy(wave_hbm, state.at[0, :, pl.ds(1, n)], load_sem.at[0]),
+        pltpu.make_async_copy(wave_hbm, state[0].at[:, pl.ds(1, n)], load_sem.at[0]),
         pltpu.make_async_copy(trap_hbm, trap, load_sem.at[1]),
         pltpu.make_async_copy(one_hbm, one, load_sem.at[2]),
         pltpu.make_async_copy(two_hbm, two, load_sem.at[3]),
         pltpu.make_async_copy(three_hbm, three, load_sem.at[4]),
         pltpu.make_async_copy(twiddle_hbm, twiddle, load_sem.at[5]),
     ]
-    for load in loads:
+    loads[0].start()
+    barrier = pltpu.get_barrier_semaphore()
+
+    def greet(d, carry):
+        pl.semaphore_signal(barrier, inc=1, device_id=in_y(d), device_id_type=MESH)
+        pl.semaphore_signal(barrier, inc=1, device_id=in_z(d), device_id_type=MESH)
+        return carry
+
+    lax.fori_loop(1, n, greet, 0)
+    for load in loads[1:]:
         load.start()
-    loads[0].wait()
+
+    groups = ((0, 2), (2, n // 2), (n // 2, n))
 
     def y_faces(s):
         up = pltpu.make_async_remote_copy(
-            src_ref=state.at[s, :, pl.ds(n, 1)], dst_ref=state.at[s, :, pl.ds(0, 1)],
+            src_ref=state[s].at[:, pl.ds(n, 1)], dst_ref=state[s].at[:, pl.ds(0, 1)],
             send_sem=halo_send.at[s, 0], recv_sem=halo_recv.at[s, 0],
             device_id=in_y(1), device_id_type=MESH,
         )
         down = pltpu.make_async_remote_copy(
-            src_ref=state.at[s, :, pl.ds(1, 1)], dst_ref=state.at[s, :, pl.ds(n + 1, 1)],
+            src_ref=state[s].at[:, pl.ds(1, 1)], dst_ref=state[s].at[:, pl.ds(n + 1, 1)],
             send_sem=halo_send.at[s, 1], recv_sem=halo_recv.at[s, 1],
             device_id=in_y(n - 1), device_id_type=MESH,
         )
         return up, down
 
-    def z_faces(s):
+    def z_faces(s, g):
+        first, end = groups[g]
+        part = pl.ds(first, end - first)
         up = pltpu.make_async_remote_copy(
-            src_ref=face_out.at[s, 1], dst_ref=face_in.at[s, 0],
-            send_sem=halo_send.at[s, 2], recv_sem=halo_recv.at[s, 2],
+            src_ref=face_out[s].at[1, part], dst_ref=face_in[s].at[0, part],
+            send_sem=halo_send.at[s, 2 + 2 * g], recv_sem=halo_recv.at[s, 2 + 2 * g],
             device_id=in_z(1), device_id_type=MESH,
         )
         down = pltpu.make_async_remote_copy(
-            src_ref=face_out.at[s, 0], dst_ref=face_in.at[s, 1],
-            send_sem=halo_send.at[s, 3], recv_sem=halo_recv.at[s, 3],
+            src_ref=face_out[s].at[0, part], dst_ref=face_in[s].at[1, part],
+            send_sem=halo_send.at[s, 3 + 2 * g], recv_sem=halo_recv.at[s, 3 + 2 * g],
             device_id=in_z(n - 1), device_id_type=MESH,
         )
         return up, down
 
+    def over_planes(g, do, together=2):
+        first, end = groups[g]
+
+        def some(q, carry):
+            js = [first + together * q + k for k in range(together)]
+            do([(j, j * (n - 1) if g == 0 else j - 1) for j in js])
+            return carry
+
+        lax.fori_loop(0, (end - first) // together, some, 0)
+
+    def keep_faces(s, j, i, plane):
+        face_out[s][0, j, i : i + 1, :] = plane[0:1]
+        face_out[s][1, j, i : i + 1, :] = plane[n - 1 : n]
+
+    loads[0].wait()
+
+    def first_faces(planes):
+        for j, y in planes:
+            for i in range(4):
+                keep_faces(0, j, i, state[0][i, y + 1])
+
+    for g in range(3):
+        over_planes(g, first_faces)
     pl.semaphore_wait(barrier, 2 * (n - 1))
-    for copy in y_faces(0):
-        copy.start()
-
-    def first_faces(y, carry):
-        for i in range(4):
-            plane = state[0, i, y + 1]
-            face_out[0, 0, i, pl.ds(y, 1), :] = plane[0:1]
-            face_out[0, 1, i, pl.ds(y, 1), :] = plane[n - 1 : n]
-        return carry
-
-    lax.fori_loop(0, n, first_faces, 0)
-    for copy in z_faces(0):
+    for copy in y_faces(0) + z_faces(0, 0) + z_faces(0, 1) + z_faces(0, 2):
         copy.start()
     loads[1].wait()
 
     row = lax.broadcasted_iota(jnp.int32, (n, size), 0)
 
-    def slope(s, y):
-        center = [state[s, i, y + 1] for i in range(4)]
+    def slope(s, j, y, components=(0, 1)):
+        center = [state[s][i, y + 1] for i in range(4)]
         density = [
             center[0] * center[0] + center[1] * center[1],
             center[2] * center[2] + center[3] * center[3],
         ]
         base = trap[y]
-        level = [
-            base + inter_self_first * density[0] + inter_cross * density[1],
-            base + inter_cross * density[0] + inter_self_second * density[1],
-        ]
-        applied = []
-        for i in range(4):
-            mid = center[i]
-            beside = state[s, i, y + 2] + state[s, i, y]
-            before = face_in[s, 0, i, pl.ds(y, 1), :]
-            after = face_in[s, 1, i, pl.ds(y, 1), :]
-            beside += jnp.where(row == 0, before, pltpu.roll(mid, 1, 0))
-            beside += jnp.where(row == n - 1, after, pltpu.roll(mid, n - 1, 0))
-            beside += pltpu.roll(mid, 1, 1) + pltpu.roll(mid, size - 1, 1)
-            applied.append(
-                level[i // 2] * mid - hopping * beside - 0.5 * rabi_rate * center[(i + 2) % 4]
-            )
-        return [applied[1], -applied[0], applied[3], -applied[2]]
-
-    for s in range(4):
-        for copy in y_faces(s) + z_faces(s):
-            copy.wait_recv()
-
-        if s < 3:
-            step = (0.5 * time_step, 0.5 * time_step, time_step)[s]
-
-            def plane(y, s=s, step=step):
-                for i, change in enumerate(slope(s, y)):
-                    new = state[0, i, y + 1] + step * change
-                    state[s + 1, i, y + 1] = new
-                    face_out[s + 1, 0, i, pl.ds(y, 1), :] = new[0:1]
-                    face_out[s + 1, 1, i, pl.ds(y, 1), :] = new[n - 1 : n]
-
-            def outer(j, carry):
-                plane(j * (n - 1))
-                return carry
-
-            def inner(y, carry):
-                plane(y)
-                return carry
-
-            lax.fori_loop(0, 2, outer, 0)
-            for copy in y_faces(s + 1):
+        change = {}
+        for c in components:
+            own, cross = ((inter_self_first, inter_cross), (inter_cross, inter_self_second))[c]
+            level = base + own * density[0] + cross * density[1]
+            applied = []
+            for i in (2 * c, 2 * c + 1):
+                mid = center[i]
+                before = face_in[s][0, j, i : i + 1, :]
+                after = face_in[s][1, j, i : i + 1, :]
+                beside = state[s][i, y + 2] + state[s][i, y]
+                beside += jnp.where(row == 0, before, pltpu.roll(mid, 1, 0))
+                beside += jnp.where(row == n - 1, after, pltpu.roll(mid, n - 1, 0))
+                beside += pltpu.roll(mid, 1, 1) + pltpu.roll(mid, size - 1, 1)
+                applied.append(
+                    level * mid - hopping * beside - 0.5 * rabi_rate * center[(i + 2) % 4]
+                )
+            change[2 * c], change[2 * c + 1] = applied[1], -applied[0]
+        return change
+
+    for s in range(3):
+        step = (0.5 * time_step, 0.5 * time_step, time_step)[s]
+
+        def advance(planes, s=s, step=step):
+            made = []
+            for j, y in planes:
+                for i, change in slope(s, j, y).items():
+                    made.append((j, y, i, state[0][i, y + 1] + step * change))
+            for j, y, i, new in made:
+                state[s + 1][i, y + 1] = new
+                keep_faces(s + 1, j, i, new)
+
+        for g in range(3):
+            for copy in z_faces(s, g) + (y_faces(s) if g == 0 else ()):
+                copy.wait_recv()
+            over_planes(g, advance)
+            for copy in (y_faces(s + 1) if g == 0 else ()) + z_faces(s + 1, g):
                 copy.start()
-            lax.fori_loop(1, n - 1, inner, 0)
-            for copy in z_faces(s + 1):
-                copy.start()
-        else:
-
-            def last(y, carry):
-                for i, change in enumerate(slope(3, y)):
-                    kept = (
-                        state[1, i, y + 1] + state[3, i, y + 1] - state[0, i, y + 1]
-                        + 2.0 * state[2, i, y + 1]
-                    )
-                    new = kept * (1.0 / 3.0) + (time_step / 6.0) * change
-                    wave_next[i, y] = new
-                    high, low = split(new)
-                    rows = pl.ds(pl.multiple_of(y * n, n), n)
-                    field[0, i // 2, rows, (i % 2) * size : (i % 2 + 1) * size] = high
-                    field[1, i // 2, rows, (i % 2) * size : (i % 2 + 1) * size] = low
-                return carry
-
-            lax.fori_loop(0, n, last, 0)
-
-    store = pltpu.make_async_copy(wave_next, next_hbm, store_sem)
-    store.start()
 
     def y_copy(ch, d):
         return pltpu.make_async_remote_copy(
@@ -273,17 +261,44 @@
 
         lax.fori_loop(1, n, one_wait, 0)
 
-    loads[2].wait()
-
-    def along_x(ch, carry):
-        c, h = ch % 2, ch // 2
-        out = product((one[0, h], one[1, h]), field[0, c], field[1, c], NT)
-        sent_y[ch] = out.reshape(n, n, size)
-        start_all(y_copy, ch)
-        got_y[ch, gy] = sent_y[ch, gy]
-        return carry
-
-    lax.fori_loop(0, CHUNKS, along_x, 0)
+    for c in range(2):
+
+        def last(planes, c=c):
+            made = []
+            for j, y in planes:
+                for i, change in slope(3, j, y, (c,)).items():
+                    kept = (
+                        state[1][i, y + 1] + state[3][i, y + 1] - state[0][i, y + 1]
+                        + 2.0 * state[2][i, y + 1]
+                    )
+                    made.append((y, i, kept * (1.0 / 3.0) + (time_step / 6.0) * change))
+            for y, i, new in made:
+                wave_next[i, y] = new
+                high, low = split(new)
+                rows = pl.ds(pl.multiple_of(y * n, n), n)
+                field[0, c, rows, (i % 2) * size : (i % 2 + 1) * size] = high
+                field[1, c, rows, (i % 2) * size : (i % 2 + 1) * size] = low
+
+        for g in range(3):
+            if c == 0:
+                for copy in z_faces(3, g) + (y_faces(3) if g == 0 else ()):
+                    copy.wait_recv()
+            over_planes(g, last)
+        if c == 0:
+            loads[2].wait()
+
+        def along_x(h, carry, c=c):
+            ch = 2 * c + h
+            out = product((one[0, h], one[1, h]), field[0, c], field[1, c], NT)
+            sent_y[ch] = out.reshape(n, n, size)
+            start_all(y_copy, ch)
+            got_y[ch, gy] = sent_y[ch, gy]
+            return carry
+
+        lax.fori_loop(0, 2, along_x, 0)
+
+    store = pltpu.make_async_copy(wave_next, next_hbm, store_sem)
+    store.start()
 
     loads[3].wait()
     loads[5].wait()
@@ -316,23 +331,25 @@
 
     loads[4].wait()
 
-    def along_z(h, carry):
-        power = None
-        for c in range(2):
-            ch = 2 * h + c
+    for c in range(2):
+
+        def along_z(h, carry, c=c):
+            ch = 2 * c + h
             arrived(z_copy, ch)
             high, low = split(got_z[ch].reshape(2 * size, size // 2))
             out = product((three[0], three[1]), high, low, NN)
             re, im = out[:size], out[size:]
             new = re * re + im * im
-            power = new if power is None else power + new
-        image_ref[h] = (power * (1.0 / float(size**3))).T
-        return carry
-
-    lax.fori_loop(0, 2, along_z, 0)
+            if c == 0:
+                power[h] = new
+            else:
+                image_ref[h] = ((power[h] + new) * (1.0 / float(size**3))).T
+            return carry
+
+        lax.fori_loop(0, 2, along_z, 0)
 
     for s in range(4):
-        for copy in y_faces(s) + z_faces(s):
+        for copy in y_faces(s) + z_faces(s, 0) + z_faces(s, 1) + z_faces(s, 2):
             copy.wait_send()
 
     def sent(j, carry):
@@ -359,15 +376,14 @@
                 jax.ShapeDtypeStruct((4, n, n, size), f32),
                 jax.ShapeDtypeStruct((2, size // 2, size), f32),
             ),
-            in_specs=[pl.BlockSpec(memory_space=pl.ANY)] * 6,
+            in_specs=[pl.BlockSpec(memory_space=pltpu.HBM)] * 6,
             out_specs=(
-                pl.BlockSpec(memory_space=pl.ANY),
+                pl.BlockSpec(memory_space=pltpu.HBM),
                 pl.BlockSpec(memory_space=pltpu.VMEM),
             ),
             scratch_shapes=[
-                pltpu.VMEM((4, 4, n + 2, n, size), f32),
-                pltpu.VMEM((4, 2, 4, n, size), f32),
-                pltpu.VMEM((4, 2, 4, n, size), f32),
+                *[pltpu.VMEM((4, n + 2, n, size), f32)] * 4,
+                *[pltpu.VMEM((2, n, 4, size), f32)] * 8,
                 pltpu.VMEM((n, n, size), f32),
                 pltpu.VMEM((4, n, n, size), f32),
                 pltpu.VMEM((2, 2, size, 2 * size), bf16),
@@ -380,17 +396,18 @@
                 pltpu.VMEM((2, size // 2, 2 * size), bf16),
                 pltpu.VMEM((CHUNKS, n, 2 * n, size // 2), f32),
                 pltpu.VMEM((CHUNKS, n, 2 * n, size // 2), f32),
+                pltpu.VMEM((2, size, size // 2), f32),
                 dma((6,)),
                 dma(()),
-                dma((4, 4)),
-                dma((4, 4)),
+                dma((4, 8)),
+                dma((4, 8)),
                 dma((CHUNKS, n)),
                 dma((CHUNKS, n)),
                 dma((CHUNKS, n)),
                 dma((CHUNKS, n)),
             ],
             compiler_params=pltpu.CompilerParams(
-                collective_id=0, has_side_effects=True, vmem_limit_bytes=48 * 1024 * 1024
+                collective_id=0, has_side_effects=True, vmem_limit_bytes=60 * 1024 * 1024
             ),
         )(wave_field.reshape(4, n, n, size), trap_field, *(jnp.asarray(a) for a in arrays))
         image = image.reshape(2, n, half, size).transpose(0, 2, 1, 3).reshape(n, n, size)

time: 84.3 us -> 75.8 us (0.90)
  local copies, waits for them, and re-layouts: 8.35 us -> 4 us
  Pallas kernels: 75 us -> 71 us
    unnamed x13 -> x1, local copies, waits for them, and re-layouts: 7.57 us -> 2.26 us
    pallas_call x1, Pallas kernels: 75 us -> 71 us  [body(): pl.pallas_call(lambda *refs: kernel(n, *refs), out_shape=(jax.ShapeDtypeS...]
    transpose x1, local copies, waits for them, and re-layouts: 0.78 us -> 1.73 us  [body(): image.reshape(2, n, half, size).transpose(0, 2, 1, 3).reshape(n, n, size)]
where the time goes in v1:
time: 75.8 us; the launch traced here: 75.7 us
  Pallas kernels  71 us (94%)
  local copies, waits for them, and re-layouts  4 us (5%)
    pallas_call x1, Pallas kernels, body(): pl.pallas_call(lambda *refs: kernel(n, *refs), out_shape=(jax.ShapeDtypeS...  71 us
    unnamed x1, local copies, waits for them, and re-layouts  2.26 us
    transpose x1, local copies, waits for them, and re-layouts, body(): image.reshape(2, n, half, size).transpose(0, 2, 1, 3).reshape(n, n, size)  1.73 us

profile of v1, /device:TPU:1, one launch (start us, length us, event | category | flops | bytes accessed | tf_op | source)
XLA Modules:
  0.0 75.7 jit_solution(11598854514308445537)
XLA Ops:
  0.6 71.0 %shard_map.77 = (f32[4,16,16,256]{3,2,1,0:T(8,128)}, f32[2,128,256]{2,1,0:T(8,128)}) custom-call(f32[4,16,16,256]{3,2,1,0:T(8,128)} %bitcast.6, f32[16,16,256]{2,1,0:T(8,128)} %refs_1_.1, bf16[2,2,256,512]{3,2,1,0:T(8,128)(2,1)} %constant.8.clone.refs_2_, bf16[2,512,512]{2,1,0:T(8,128)(2,1)} %constant.9.clone.refs_3_, ...), custom_call_target="tpu_custom_call" | custom-call | tf_op jit(solution)/shard_map/pallas_call | solution.py:373
  71.7 1.7 %copy.8 = f32[2,8,16,256]{3,2,1,0:T(8,128)} copy(f32[2,8,16,256]{3,1,2,0:T(8,128)} %bitcast.8) | data formatting | bytes 524288 | tf_op jit(solution)/shard_map/transpose | solution.py:413
  73.4 2.3 %copy.10 = f32[2,2,16,16,256]{4,3,2,1,0:T(8,128)} copy(f32[2,2,16,16,256]{4,3,2,1,0:T(8,128)} %bitcast.7) | data formatting | bytes 2097152

commit v2 on v1

--- a/solution.py
+++ b/solution.py
@@ -407,7 +407,7 @@
                 dma((CHUNKS, n)),
             ],
             compiler_params=pltpu.CompilerParams(
-                collective_id=0, has_side_effects=True, vmem_limit_bytes=60 * 1024 * 1024
+                collective_id=0, has_side_effects=True, vmem_limit_bytes=52 * 1024 * 1024
             ),
         )(wave_field.reshape(4, n, n, size), trap_field, *(jnp.asarray(a) for a in arrays))
         image = image.reshape(2, n, half, size).transpose(0, 2, 1, 3).reshape(n, n, size)

time: 75.8 us -> 74.4 us (0.982)
  Pallas kernels: 71 us -> 70.1 us
    pallas_call x1, Pallas kernels: 71 us -> 70.1 us  [body(): pl.pallas_call(lambda *refs: kernel(n, *refs), out_shape=(jax.ShapeDtypeS...]
    transpose x1, local copies, waits for them, and re-layouts: 1.73 us -> 0.78 us  [body(): image.reshape(2, n, half, size).transpose(0, 2, 1, 3).reshape(n, n, size)]
    unnamed x1 -> x5, local copies, waits for them, and re-layouts: 2.26 us -> 2.67 us
where the time goes in v2:
time: 74.4 us; the launch traced here: 74.2 us
  Pallas kernels  70.1 us (94%)
  local copies, waits for them, and re-layouts  3.45 us (5%)
    pallas_call x1, Pallas kernels, body(): pl.pallas_call(lambda *refs: kernel(n, *refs), out_shape=(jax.ShapeDtypeS...  70.1 us
    unnamed x5, local copies, waits for them, and re-layouts  2.67 us

profile of v2, /device:TPU:1, one launch (start us, length us, event | category | flops | bytes accessed | tf_op | source)
XLA Modules:
  0.0 74.2 jit_solution(13629798404132932829)
XLA Ops:
  0.6 0.0 copy-start
  0.6 0.9 %copy-done = f32[16,16,256]{2,1,0:T(8,128)S(1)} copy-done((f32[16,16,256]{2,1,0:T(8,128)S(1)}, f32[16,16,256]{2,1,0:T(8,128)}, u32[]{:S(2)}) %copy-start) | copy-done | bytes 262168
  1.6 0.0 copy-start.1
  1.6 0.8 %copy-done.1 = f32[16,2,256]{2,1,0:T(2,128)S(1)} copy-done((f32[16,2,256]{2,1,0:T(2,128)S(1)}, f32[16,2,256]{2,1,0:T(2,128)}, u32[]{:S(2)}) %copy-start.1) | copy-done | bytes 32792
  2.3 70.1 %shard_map.77 = (f32[4,16,16,256]{3,2,1,0:T(8,128)S(1)}, f32[2,128,256]{2,1,0:T(8,128)S(1)}) custom-call(f32[4,16,16,256]{3,2,1,0:T(8,128)} %bitcast.8, f32[16,16,256]{2,1,0:T(8,128)S(1)} %copy-done, bf16[2,2,256,512]{3,2,1,0:T(8,128)(2,1)} %constant.8.clone.refs_2_, bf16[2,512,512]{2,1,0:T(8,128)(2,1)} %constant.9.clone.refs_3_, ...), custom_call_target="tpu_custom_call" | custom-call | tf_op jit(solution)/shard_map/pallas_call | solution.py:373
  72.4 0.8 %copy.8 = f32[2,8,16,256]{3,2,1,0:T(8,128)} copy(f32[2,8,16,256]{3,1,2,0:T(8,128)S(1)} %bitcast.7) | data formatting | bytes 524288 | tf_op jit(solution)/shard_map/transpose | solution.py:413
  73.2 1.0 %copy.10 = f32[2,2,16,16,256]{4,3,2,1,0:T(8,128)} copy(f32[2,2,16,16,256]{4,3,2,1,0:T(8,128)S(1)} %bitcast.6) | data formatting | bytes 2097152
Async XLA Ops:
  0.6 1.0 %copy-start = (f32[16,16,256]{2,1,0:T(8,128)S(1)}, f32[16,16,256]{2,1,0:T(8,128)}, u32[]{:S(2)}) copy-start(f32[16,16,256]{2,1,0:T(8,128)} %refs_1_.1) | copy-start | bytes 786436
  1.6 0.8 %copy-start.1 = (f32[16,2,256]{2,1,0:T(2,128)S(1)}, f32[16,2,256]{2,1,0:T(2,128)}, u32[]{:S(2)}) copy-start(f32[16,2,256]{2,1,0:T(2,128)} %constant.11.clone.refs_5_) | copy-start | bytes 98308

commit v3 on v2

--- a/solution.py
+++ b/solution.py
@@ -44,8 +44,9 @@
     three = full.reshape(2, 2, size, n, n).transpose(0, 2, 3, 1, 4).reshape(2 * size, 2 * size)
     turn = 2.0 * np.pi * (j[:, None] * j[None, :]) / size
     turn = np.repeat(turn, n, axis=1)
-    twiddle = np.stack([np.cos(turn), np.sin(turn)], axis=1).astype(np.float32)
-    return in_two(one), in_two(two), in_two(three), twiddle
+    twiddle = np.stack([np.cos(turn), np.sin(turn)], axis=1)
+    two = np.concatenate([two, twiddle.reshape(n, 2 * size)])
+    return in_two(one), in_two(two), in_two(three)
 
 
 def fourier(values):
@@ -90,7 +91,7 @@
 
 
 def kernel(
-    n, wave_hbm, trap_hbm, one_hbm, two_hbm, three_hbm, twiddle_hbm,
+    n, wave_hbm, trap_hbm, one_hbm, two_hbm, three_hbm,
     next_hbm, image_ref,
     state0, state1, state2, state3, out0, out1, out2, out3, in0, in1, in2, in3, trap, wave_next, field, one, two, three, twiddle,
     sent_y, got_y, mixed, sent_z, got_z, power,
@@ -113,7 +114,6 @@
         pltpu.make_async_copy(one_hbm, one, load_sem.at[2]),
         pltpu.make_async_copy(two_hbm, two, load_sem.at[3]),
         pltpu.make_async_copy(three_hbm, three, load_sem.at[4]),
-        pltpu.make_async_copy(twiddle_hbm, twiddle, load_sem.at[5]),
     ]
     loads[0].start()
     barrier = pltpu.get_barrier_semaphore()
@@ -301,19 +301,20 @@
     store.start()
 
     loads[3].wait()
-    loads[5].wait()
+    twiddle[...] = two[0, 2 * size :].astype(jnp.float32) + two[1, 2 * size :].astype(jnp.float32)
 
     def along_y(ch, carry):
         arrived(y_copy, ch)
         lanes = size // 2
         for part in range(2):
             at = slice(part * lanes, (part + 1) * lanes)
+            beyond = slice(size + part * lanes, size + (part + 1) * lanes)
             values = [(got_y[ch, s, 0:half, at], got_y[ch, s, half:n, at]) for s in range(n)]
             values = fourier(values)
             for b in range(0, n, 2):
                 turned = []
                 for k in (b, b + 1):
-                    (re, im), cos, sin = values[k], twiddle[k, 0:1, at], twiddle[k, 1:2, at]
+                    (re, im), cos, sin = values[k], twiddle[k : k + 1, at], twiddle[k : k + 1, beyond]
                     turned.append((re * cos + im * sin, im * cos - re * sin))
                 for p in range(2):
                     both = jnp.concatenate([turned[0][p], turned[1][p]], axis=0)
@@ -321,7 +322,7 @@
                     to = slice(p * size + part * lanes, p * size + (part + 1) * lanes)
                     mixed[0, b * half : (b + 2) * half, to] = high
                     mixed[1, b * half : (b + 2) * half, to] = low
-        out = product((two[0], two[1]), mixed[0], mixed[1], NT)
+        out = product((two[0, : 2 * size], two[1, : 2 * size]), mixed[0], mixed[1], NT)
         sent_z[ch] = out.reshape(n, 2 * n, size // 2)
         start_all(z_copy, ch)
         got_z[ch, gz] = sent_z[ch, gz]
@@ -376,7 +377,7 @@
                 jax.ShapeDtypeStruct((4, n, n, size), f32),
                 jax.ShapeDtypeStruct((2, size // 2, size), f32),
             ),
-            in_specs=[pl.BlockSpec(memory_space=pltpu.HBM)] * 6,
+            in_specs=[pl.BlockSpec(memory_space=pltpu.HBM)] * 5,
             out_specs=(
                 pl.BlockSpec(memory_space=pltpu.HBM),
                 pl.BlockSpec(memory_space=pltpu.VMEM),
@@ -388,16 +389,16 @@
                 pltpu.VMEM((4, n, n, size), f32),
                 pltpu.VMEM((2, 2, size, 2 * size), bf16),
                 pltpu.VMEM((2, 2, size, 2 * size), bf16),
+                pltpu.VMEM((2, 2 * size + n, 2 * size), bf16),
                 pltpu.VMEM((2, 2 * size, 2 * size), bf16),
-                pltpu.VMEM((2, 2 * size, 2 * size), bf16),
-                pltpu.VMEM((n, 2, size), f32),
+                pltpu.VMEM((n, 2 * size), f32),
                 pltpu.VMEM((CHUNKS, n, n, size), f32),
                 pltpu.VMEM((CHUNKS, n, n, size), f32),
                 pltpu.VMEM((2, size // 2, 2 * size), bf16),
                 pltpu.VMEM((CHUNKS, n, 2 * n, size // 2), f32),
                 pltpu.VMEM((CHUNKS, n, 2 * n, size // 2), f32),
                 pltpu.VMEM((2, size, size // 2), f32),
-                dma((6,)),
+                dma((5,)),
                 dma(()),
                 dma((4, 8)),
                 dma((4, 8)),
@@ -409,7 +410,7 @@
             compiler_params=pltpu.CompilerParams(
                 collective_id=0, has_side_effects=True, vmem_limit_bytes=52 * 1024 * 1024
             ),
-        )(wave_field.reshape(4, n, n, size), trap_field, *(jnp.asarray(a) for a in arrays))
+        )(wave_field.reshape(4, n, n, size), pltpu.with_memory_space_constraint(trap_field, pltpu.HBM), *(jnp.asarray(a) for a in arrays))
         image = image.reshape(2, n, half, size).transpose(0, 2, 1, 3).reshape(n, n, size)
         return wave_next.reshape(2, 2, n, n, size), image
 

time: 74.4 us -> 72.8 us (0.978)
  local copies, waits for them, and re-layouts: 3.45 us -> 1.75 us
    unnamed x5 -> x1, local copies, waits for them, and re-layouts: 2.67 us -> 0.97 us
where the time goes in v3:
time: 72.8 us; the launch traced here: 72.7 us
  Pallas kernels  70.3 us (97%)
  local copies, waits for them, and re-layouts  1.75 us (2%)
    pallas_call x1, Pallas kernels, body(): pl.pallas_call(lambda *refs: kernel(n, *refs), out_shape=(jax.ShapeDtypeS...  70.3 us

profile of v3, /device:TPU:1, one launch (start us, length us, event | category | flops | bytes accessed | tf_op | source)
XLA Modules:
  0.0 72.7 jit_solution(9438482223442906770)
XLA Ops:
  0.6 70.3 %shard_map.68 = (f32[4,16,16,256]{3,2,1,0:T(8,128)S(1)}, f32[2,128,256]{2,1,0:T(8,128)S(1)}) custom-call(f32[4,16,16,256]{3,2,1,0:T(8,128)} %bitcast.8, f32[16,16,256]{2,1,0:T(8,128)} %refs_1_.1, bf16[2,2,256,512]{3,2,1,0:T(8,128)(2,1)} %constant.6.clone.refs_2_, bf16[2,528,512]{2,1,0:T(8,128)(2,1)} %constant.7.clone.refs_3_, ...), custom_call_target="tpu_custom_call" | custom-call | tf_op jit(solution)/shard_map/pallas_call | solution.py:374
  71.0 0.8 %copy.7 = f32[2,8,16,256]{3,2,1,0:T(8,128)} copy(f32[2,8,16,256]{3,1,2,0:T(8,128)S(1)} %bitcast.7) | data formatting | bytes 524288 | tf_op jit(solution)/shard_map/transpose | solution.py:414
  71.8 1.0 %copy.9 = f32[2,2,16,16,256]{4,3,2,1,0:T(8,128)} copy(f32[2,2,16,16,256]{4,3,2,1,0:T(8,128)S(1)} %bitcast.6) | data formatting | bytes 2097152

commit v4 on v3

--- a/solution.py
+++ b/solution.py
@@ -159,6 +159,8 @@
 
     def over_planes(g, do, together=2):
         first, end = groups[g]
+        if (end - first) % 4 == 0:
+            together = 4
 
         def some(q, carry):
             js = [first + together * q + k for k in range(together)]

time: 72.8 us -> 72.8 us (level)
  no operation moved by 1% of the time
where the time goes in v4:
time: 72.8 us; the launch traced here: 72.7 us
  Pallas kernels  70.3 us (97%)
  local copies, waits for them, and re-layouts  1.75 us (2%)
    pallas_call x1, Pallas kernels, body(): pl.pallas_call(lambda *refs: kernel(n, *refs), out_shape=(jax.ShapeDtypeS...  70.3 us

profile of v4, /device:TPU:1, one launch (start us, length us, event | category | flops | bytes accessed | tf_op | source)
XLA Modules:
  0.0 72.7 jit_solution(10604316883613498460)
XLA Ops:
  0.6 70.3 %shard_map.68 = (f32[4,16,16,256]{3,2,1,0:T(8,128)S(1)}, f32[2,128,256]{2,1,0:T(8,128)S(1)}) custom-call(f32[4,16,16,256]{3,2,1,0:T(8,128)} %bitcast.8, f32[16,16,256]{2,1,0:T(8,128)} %refs_1_.1, bf16[2,2,256,512]{3,2,1,0:T(8,128)(2,1)} %constant.6.clone.refs_2_, bf16[2,528,512]{2,1,0:T(8,128)(2,1)} %constant.7.clone.refs_3_, ...), custom_call_target="tpu_custom_call" | custom-call | tf_op jit(solution)/shard_map/pallas_call | solution.py:376
  70.9 0.8 %copy.7 = f32[2,8,16,256]{3,2,1,0:T(8,128)} copy(f32[2,8,16,256]{3,1,2,0:T(8,128)S(1)} %bitcast.7) | data formatting | bytes 524288 | tf_op jit(solution)/shard_map/transpose | solution.py:416
  71.7 1.0 %copy.9 = f32[2,2,16,16,256]{4,3,2,1,0:T(8,128)} copy(f32[2,2,16,16,256]{4,3,2,1,0:T(8,128)S(1)} %bitcast.6) | data formatting | bytes 2097152
